TPU v7x, 32 devices: a whole 2x2x4 slice. The times are simulated.
32 devices in a mesh: gx: 4 (over z), gy: 2 (over x), gz: 4 (over y, core).
Axes of the slice: x: 2, y: 2, z: 4, core: 2. Of those that a mesh axis runs over, the one named last changes fastest.
Arguments:
- load_currents: float32 [24, 16, 32, 256], P(None, 'gz', 'gx', 'gy')
- cond_rows: float32 [16, 32, 256], P('gz', 'gx', 'gy'), may hold values from 0.5 to 2
- cond_cols: float32 [16, 32, 256], P('gz', 'gx', 'gy'), may hold values from 0.5 to 2
- cond_vias: float32 [16, 32, 256], P('gz', 'gx', 'gy'), may hold values from 0.5 to 2
- ground: float32 [16, 32, 256], P('gz', 'gx', 'gy'), may hold values from 0.02 to 0.5
- via_offset: int32 [16], replicated, may hold values from -1 to 1, as said below
Outputs:
- basis_q: float32 [96, 16, 32, 256], P(None, 'gz', 'gx', 'gy')
- factor_r: float32 [96, 96], replicated
Inputs may be any that keep to these rules, and one draw needn't show every extreme that they name: `via_offset`: in every aligned group of three layers (layers 3 k, 3 k + 1, 3 k + 2) the offsets -1, 0 and 1 appear once each.
All inputs are finite; a program needn't handle non-finite values.
Results may differ from a plain program's by a relative error of at most 0.0003.
Values sent between devices are 32-bit elements; how exact they have to be, the bound alone decides.
No kernel may reach another device: no remote copies, remote signals or barrier semaphores. Data moves between devices by JAX's collectives and lax.ppermute only.
A program may use at most 64 MiB of HBM per device.

v0:
```python
import functools

import jax
import jax.numpy as jnp
from jax import lax
from jax.experimental import pallas as pl
from jax.experimental.pallas import tpu as pltpu
from jax.sharding import PartitionSpec as P

POWERS = 4


newton_shifts = (15.4, 0.6, 11.7, 4.3)
basis_scale = 0.125

VMEM = pl.BlockSpec(memory_space=pltpu.VMEM)
SMEM = pl.BlockSpec(memory_space=pltpu.SMEM)
HBM = pl.BlockSpec(memory_space=pltpu.HBM)
PARAMS = pltpu.CompilerParams(vmem_limit_bytes=32 * 1024 * 1024)
FIRST = pltpu.CompilerParams(vmem_limit_bytes=60 * 1024 * 1024)

COEFS = 4
TILE = 8
CORNERS = ((1, 3), (1, 2), (1, 1), (2, 2), (2, 1), (3, 1))


def positions(shape):
    sub = lax.broadcasted_iota(jnp.int32, shape, 0)
    lane = lax.broadcasted_iota(jnp.int32, shape, 1)
    return sub, lane


def coefs_at(ref, start, i):
    place = start + COEFS * (i // 2) * 2
    tile = ref[place : place + TILE, :]
    return pltpu.roll(tile, COEFS, 0) if i % 2 else tile


def edges_kernel(
    load_ref, rows_ref, cols_ref, vias_ref, ground_ref, offset_ref,
    first_ref, second_ref, tile_ref, flat_ref, shift_ref, fields_in, coefs_in, sems,
):
    slabs, _, cols = tile_ref.shape
    fields = load_ref.shape[0] // slabs
    layers, rows, _ = rows_ref.shape
    depth = POWERS
    half = rows // 2
    total_layers = offset_ref.shape[0]
    copies = [
        pltpu.make_async_copy(ref, coefs_in.at[i], sems.at[i])
        for i, ref in enumerate((rows_ref, cols_ref, vias_ref, ground_ref))
    ]
    copies.append(pltpu.make_async_copy(load_ref, fields_in, sems.at[COEFS]))
    for copy in copies:
        copy.start()
    gx, gy, gz = (lax.axis_index(name) for name in ("gx", "gy", "gz"))
    last_row = jnp.where(gx == lax.axis_size("gx") - 1, rows - 1, rows)
    last_col = jnp.where(gy == lax.axis_size("gy") - 1, cols - 1, cols)
    sub, lane = positions((TILE, cols))
    for e in range(shift_ref.shape[0]):
        layer = gz * layers + e - depth
        inside = (layer >= 0) & (layer < total_layers)
        value = jnp.where(inside, offset_ref[jnp.clip(layer, 0, total_layers - 1)], 0)
        shift_ref[e] = jnp.broadcast_to(value, (TILE, cols))
    for copy in copies:
        copy.wait()

    def joined(one, two):
        return jnp.where(sub < COEFS, one, pltpu.roll(two, COEFS, 0))

    for l in range(layers):
        layer = gz * layers + l
        target = gy * cols + lane + shift_ref[depth + l]
        via_ok = (target >= 0) & (target < cols * lax.axis_size("gy"))
        via_ok = via_ok & (jnp.broadcast_to(layer, lane.shape) < total_layers - 1)
        four = (
            jnp.where(sub == last_row, 0.0, coefs_in[0, l]),
            jnp.where(lane == last_col, 0.0, coefs_in[1, l]),
            jnp.where(via_ok, coefs_in[2, l], 0.0),
            coefs_in[3, l],
        )
        for r in range(rows):
            slab = l * rows + r
            value = jnp.zeros((TILE, cols), jnp.float32)
            for c in range(COEFS):
                value = jnp.where(sub == c, jnp.broadcast_to(four[c][r : r + 1, :], (TILE, cols)), value)
            tile_ref[slab] = value
    for i in range(0, slabs, 2):
        flat_ref[COEFS * i : COEFS * i + TILE, :] = joined(tile_ref[i], tile_ref[i + 1])
    even = lax.rem(gx, 2) == 0
    for ref, start in ((first_ref, jnp.where(even, half, 0)), (second_ref, jnp.where(even, 0, half))):
        for l in range(layers):
            for i in range(half):
                slab = l * rows + start + i
                at = l * half + i
                for f in range(0, fields, TILE):
                    tile = fields_in[pl.ds(f * slabs + slab, TILE, stride=slabs), :]
                    ref[at * fields + f : at * fields + f + TILE, :] = tile
                if i % 2 == 0:
                    place = layers * half * fields + COEFS * at
                    ref[place : place + TILE, :] = joined(tile_ref[slab], tile_ref[slab + 1])


def own_kernel(load_ref, tile_ref, block_ref):
    slabs, planes, _ = block_ref.shape
    for slab in range(slabs):
        for f in range(0, planes - TILE, TILE):
            block_ref[slab, f : f + TILE, :] = load_ref[pl.ds(f * slabs + slab, TILE, stride=slabs), :]
        block_ref[slab, planes - TILE :, :] = tile_ref[slab]


def corners_kernel(first_ref, second_ref, flat_ref, after_ref, before_ref, one_ref, two_ref, *, layers):
    slabs, planes, cols = after_ref.shape
    fields = planes - TILE
    half = slabs // layers
    count = len(CORNERS)
    sub, _ = positions((TILE, cols))
    even_row = jnp.broadcast_to(lax.rem(lax.axis_index("gx"), 2), (TILE, cols)) == 0
    even_layer = jnp.broadcast_to(lax.rem(lax.axis_index("gz"), 2), (TILE, cols)) == 0
    row_block = jnp.broadcast_to(lax.axis_index("gx"), (TILE, cols))
    has_prev, has_next = row_block > 0, row_block < lax.axis_size("gx") - 1
    for f in range(0, planes, TILE):
        after, before = [], []
        for i in range(slabs):
            if f < fields:
                first, second = (ref[i * fields + f : i * fields + f + TILE, :] for ref in (first_ref, second_ref))
            else:
                first, second = (coefs_at(ref, slabs * fields, i) for ref in (first_ref, second_ref))
            after.append(jnp.where(has_prev, jnp.where(even_row, second, first), 0.0))
            before.append(jnp.where(has_next, jnp.where(even_row, first, second), 0.0))
            after_ref[i, f : f + TILE, :] = after[i]
            before_ref[i, f : f + TILE, :] = before[i]
        ones, twos = [], []
        for source, step in ((after, -1), (before, 1)):
            for dz, dx in CORNERS:
                row = half - dx if step < 0 else dx - 1
                up, down = source[(layers - dz) * half + row], source[(dz - 1) * half + row]
                ones.append(jnp.where(even_layer, up, down))
                twos.append(jnp.where(even_layer, down, up))
        for ref, values in ((one_ref, ones), (two_ref, twos)):
            if f < fields:
                for i, value in enumerate(values):
                    ref[i * fields + f : i * fields + f + TILE, :] = value
            else:
                for i in range(0, 2 * count, 2):
                    place = 2 * count * fields + COEFS * i
                    pair = jnp.where(sub < COEFS, values[i], pltpu.roll(values[i + 1], COEFS, 0))
                    ref[place : place + TILE, :] = pair
    for ref in (one_ref, two_ref):
        place = 2 * count * planes - 2 * count * (TILE - COEFS)
        ref[place : place + flat_ref.shape[0], :] = flat_ref[...]


def slabs_of(e, layers, rows, planes, corners, inner, block, after, before, one, two, corner_one=None, corner_two=None):
    depth, half, count = POWERS, rows // 2, len(CORNERS)
    cols = block.shape[2] if block is not None else corner_one.shape[1]
    fields, slabs = planes - TILE, layers * rows

    def plain(ref, slab):
        return lambda f: ref[slab, f : f + TILE, :]

    def chosen(read, one, two):
        place = jnp.broadcast_to(lax.axis_index("gz"), (TILE, cols))
        even = lax.rem(place, 2) == 0
        there = place > 0 if e < depth else place < lax.axis_size("gz") - 1
        return lambda f: jnp.where(there, jnp.where(even, read(one, f), read(two, f)), 0.0)

    def home(slab):
        return lambda ref, f: ref[pl.ds(f * slabs + slab, TILE, stride=slabs), :]

    def home_coefs(slab):
        return lambda ref, f: coefs_at(ref, 2 * count * (fields + COEFS), slab)

    def corner(i):
        def read(ref, f):
            if f < fields:
                return ref[i * fields + f : i * fields + f + TILE, :]
            return coefs_at(ref, 2 * count * fields, i)

        return read

    tiles = [f for f in range(0, planes, TILE)]
    found = []
    if depth <= e < depth + layers:
        l = e - depth
        if inner:
            found += [(depth + r, plain(block, l * rows + r), tiles) for r in range(rows)]
            for i in range(half):
                found.append((i, plain(after, l * half + i), tiles))
                found.append((depth + rows + i, plain(before, l * half + i), tiles))
        return found
    if e < depth:
        pair, corner_pair, first, distance = (two, one), (corner_two, corner_one), 0, depth - e
    else:
        pair, corner_pair = (one, two), (corner_one, corner_two)
        first, distance = depth + layers, e - depth - layers + 1
    for r in range(rows):
        slab = (e - first) * rows + r
        if inner:
            found.append((depth + r, chosen(home(slab), *pair), tiles[:-1]))
        if corners:
            found.append((depth + r, chosen(home_coefs(slab), *corner_pair), tiles[-1:]))
    for i, (dz, dx) in enumerate(CORNERS):
        if dz == distance and corners:
            found.append((depth - dx, chosen(corner(i), *corner_pair), tiles))
            found.append((depth + rows - 1 + dx, chosen(corner(count + i), *corner_pair), tiles))
    return found


def inner_kernel(*refs, layers, rows):
    sources, edge_ref = refs[:5], refs[5]
    high, planes, cols = edge_ref.shape
    depth = POWERS
    group = 2 * depth
    _, lane = positions((TILE, cols))
    for e in range(high):
        found = slabs_of(e, layers, rows, planes, False, True, *sources)
        for f in range(0, planes, TILE):
            total = jnp.zeros((TILE, cols), jnp.float32)
            for row, read, tiles in found:
                if f in tiles:
                    moved = pltpu.roll(read(f), (group * row + depth) % cols, 1)
                    total = jnp.where((lane >= group * row) & (lane < group * row + group), moved, total)
            edge_ref[e, f : f + TILE, :] = total


def sides_kernel(inner_ref, one_ref, two_ref, edge_ref, *out_refs, layers, rows, pair):
    high, planes, cols = edge_ref.shape
    depth = POWERS
    group = 2 * depth
    _, lane = positions((TILE, cols))
    early = lax.rem(lane, group) < depth
    gy = jnp.broadcast_to(lax.axis_index("gy"), (TILE, cols))
    for f in range(0, planes, TILE):
        here = slice(f, f + TILE)
        edges = []
        for e in range(high):
            total = inner_ref[e, here, :]
            for row, read, tiles in slabs_of(e, layers, rows, planes, True, False, None, None, None, None, None, one_ref, two_ref):
                if f in tiles:
                    moved = pltpu.roll(read(f), (group * row + depth) % cols, 1)
                    total = jnp.where((lane >= group * row) & (lane < group * row + group), moved, total)
            edge_ref[e, here, :] = total
            edges.append(total)
        for t in range(high // 2):
            one, two = edges[2 * t], edges[2 * t + 1]
            up = jnp.where(early, one, pltpu.roll(two, depth, 1))
            down = jnp.where(early, pltpu.roll(one, cols - depth, 1), two)
            if pair:
                out_refs[0][t, here, :] = jnp.where(gy == 0, up, down)
            else:
                out_refs[0][t, here, :] = up
                out_refs[1][t, here, :] = down


def assemble_kernel(*refs, layers, rows):
    sources, start_ref = refs[:7], refs[7]
    high, _, planes, _ = start_ref.shape
    for e in range(high):
        for row, read, tiles in slabs_of(e, layers, rows, planes, True, True, *sources):
            for f in tiles:
                start_ref[e, row, f : f + TILE, :] = read(f)


def powers_kernel(*refs, fields, layers, rows, pair):
    gots = 1 if pair else 2
    start_ref, edge_ref, got_refs, shift_ref = refs[0], refs[1], refs[2 : 2 + gots], refs[2 + gots]
    basis_ref, keep_ref, send_ref, power_ref, coef_ref, strip_ref, strip_coef_ref, border_ref, sum_ref = refs[3 + gots :]
    high, tall, planes, cols = start_ref.shape
    depth = POWERS
    group = 2 * depth
    order = depth * fields
    tiles = range(0, fields, TILE)
    _, lane = positions((TILE, cols))
    gy = lax.axis_index("gy")

    def masks(e):
        shift = shift_ref[e]
        return shift == 0, shift > 0

    def from_above(seen, mask):
        left, centre, right = seen
        return jnp.where(mask[0], centre, jnp.where(mask[1], right, left))

    def from_below(seen, mask):
        left, centre, right = seen
        return jnp.where(mask[0], centre, jnp.where(mask[1], left, right))

    def around(tile):
        return pltpu.roll(tile, 1, 1), tile, pltpu.roll(tile, cols - 1, 1)

    def spread(tile, c):
        return jnp.broadcast_to(tile[c : c + 1, :], (TILE, cols))

    def put_factors(put, tile, row_above, seen, seen_below, mask):
        down, right, upper, ground = (spread(tile, c) for c in range(COEFS))
        up = spread(row_above, 0)
        left = spread(seen[0], 1)
        lower = from_below([spread(x, 2) for x in seen_below], mask)
        diagonal = ground + down + up + right + left + upper + lower
        for i, value in enumerate((down, up, right, left, upper, lower, diagonal)):
            put(i, value * basis_scale)

    def step(factors, theta, seen, up, down, above, below):
        value = (factors[6] - theta) * seen[1]
        value = value - (factors[0] * down + factors[1] * up)
        value = value - (factors[2] * seen[2] + factors[3] * seen[0])
        return value - (factors[4] * above + factors[5] * below)

    thetas = [shift * basis_scale for shift in newton_shifts]

    early = lax.rem(lane, group) < depth
    if pair:
        first_side = jnp.where(gy == 0, 1, 0)
        last_side = first_side + 1
    else:
        first_side, last_side = 0, 2

    @pl.loop(first_side, last_side)
    def _(side):
        left_side = jnp.broadcast_to(side, (TILE, cols)) == 0
        from_edge = early != left_side
        for e in range(high):
            for f in range(0, planes, TILE):
                here = slice(f, f + TILE)
                outer = got_refs[0][e // 2, here, :]
                if not pair:
                    outer = jnp.where(left_side, outer, got_refs[1][e // 2, here, :])
                if e % 2 == 0:
                    outer = jnp.where(left_side, outer, pltpu.roll(outer, depth, 1))
                else:
                    outer = jnp.where(left_side, pltpu.roll(outer, cols - depth, 1), outer)
                strip_ref[side, 0, e, here, :] = jnp.where(from_edge, edge_ref[e, here, :], outer)
        raw = [strip_ref[side, 0, e, fields : fields + TILE, :] for e in range(high)]
        seen = [around(tile) for tile in raw]
        for e in range(1, high - 1):

            def put(i, value, e=e):
                strip_coef_ref[side, i, e] = value

            put_factors(put, raw[e], pltpu.roll(raw[e], group, 1), seen[e], seen[e - 1], masks(e - 1))
        for k in range(1, depth):
            reach = depth - k
            looks = {}

            def look(e, f, k=k, looks=looks):
                if (e, f) not in looks:
                    looks[e, f] = around(strip_ref[side, k - 1, e, f : f + TILE, :])
                return looks[e, f]

            for e in range(depth - reach, depth + layers + reach):
                factors = [strip_coef_ref[side, i, e] for i in range(7)]
                over, under = masks(e), masks(e - 1)
                for f in tiles:
                    here = look(e, f)
                    strip_ref[side, k, e, f : f + TILE, :] = step(
                        factors,
                        thetas[k - 1],
                        here,
                        pltpu.roll(here[1], group, 1),
                        pltpu.roll(here[1], cols - group, 1),
                        from_above(look(e + 1, f), over),
                        from_below(look(e - 1, f), under),
                    )

    gy_lane = jnp.broadcast_to(gy, (TILE, cols))
    on_left = (lax.rem(lane, group) == depth - 1) & (gy_lane > 0)
    on_right = (lax.rem(lane, group) == depth - 2) & (gy_lane < lax.axis_size("gy") - 1)

    @pl.loop(0, high)
    def _(e):
        for k in range(depth):
            for f in range(0, planes if k == 0 else fields, TILE):
                here = slice(f, f + TILE)
                right = jnp.where(on_right, pltpu.roll(strip_ref[1, k, e, here, :], cols - 2, 1), 0.0)
                border_ref[k, e, here, :] = jnp.where(on_left, strip_ref[0, k, e, here, :], right)

    leftmost, rightmost = lane == 0, lane == cols - 1

    def looked(k, e, row, f):
        here = slice(f, f + TILE)
        tile = start_ref[e, row, here, :] if k == 0 else power_ref[k - 1, e, row, here, :]
        turn = (2 * cols - group * row - depth + 1) % cols
        outer = pltpu.roll(border_ref[k, e, here, :], turn, 1)
        left, _, right = around(tile)
        return jnp.where(leftmost, outer, left), tile, jnp.where(rightmost, outer, right)

    def by_rows(reach, body):
        for r in range(rows):
            body(depth + r, depth - reach, depth + layers + reach)

        for dx in range(1, reach + 1):
            for row in (depth - dx, depth + rows - 1 + dx):
                body(row, depth - reach + dx, depth + layers + reach - dx)

    def factors_of_row(row, first, last):
        seen = {e: looked(0, e, row, fields) for e in range(first - 1, last)}
        for e in range(first, last):

            def put(i, value, e=e):
                coef_ref[i, e, row] = value

            above_row = start_ref[e, row - 1, fields : fields + TILE, :]
            put_factors(put, seen[e][1], above_row, seen[e], seen[e - 1], masks(e - 1))

    by_rows(depth - 1, factors_of_row)

    for k in range(1, depth + 1):

        def advance(row, first, last, k=k):
            source = start_ref if k == 1 else power_ref.at[k - 2]
            below = {f: from_below(looked(k - 1, first - 1, row, f), masks(first - 1)) for f in tiles}
            centre = {f: looked(k - 1, first, row, f) for f in tiles}
            for e in range(first, last):
                factors = [coef_ref[i, e, row] for i in range(7)]
                mask = masks(e)
                for f in tiles:
                    here = slice(f, f + TILE)
                    upper = looked(k - 1, e + 1, row, f)
                    value = step(
                        factors,
                        thetas[k - 1],
                        centre[f],
                        source[e, row - 1, here, :],
                        source[e, row + 1, here, :],
                        from_above(upper, mask),
                        below[f],
                    )
                    below[f], centre[f] = from_below(centre[f], mask), upper
                    if k < depth:
                        power_ref[k - 1, e, row, here, :] = value
                    if first == k and depth <= e < depth + layers:
                        slab = (e - depth) * rows + row - depth
                        place = slab * order + (k - 1) * fields + f
                        basis_ref[place : place + TILE, :] = value

        if k < depth:
            by_rows(depth - k, advance)

    def share(r):
        value = None
        for l in range(0, layers, 2):
            places = [((l + i) * rows + r) * order for i in range(2)]
            wide = jnp.concatenate([basis_ref[place : place + order, :] for place in places], axis=1)
            product = lax.dot_general(
                wide, wide, (((1,), (1,)), ((), ())),
                precision=lax.Precision.HIGHEST, preferred_element_type=jnp.float32,
            )
            value = product if value is None else value + product
        return value

    advance(depth, depth, depth + layers)
    for r in range(1, rows):
        total = share(r - 1) if r == 1 else total + share(r - 1)
        advance(depth + r, depth, depth + layers)
    total = total + share(rows - 1)
    sum_ref[...] = total
    half = order // 2
    odd = lax.rem(lax.axis_index("gz"), 2)
    keep_ref[...] = sum_ref[pl.ds(pl.multiple_of(odd * half, TILE), half), :]
    send_ref[...] = sum_ref[pl.ds(pl.multiple_of((1 - odd) * half, TILE), half), :]


def eliminate(tiles, order, step):
    width = tiles[0].shape[1]
    lane = lax.broadcasted_iota(jnp.int32, (8, width), 1)
    sub = lax.broadcasted_iota(jnp.int32, (8, width), 0)
    spread = lambda value: jnp.broadcast_to(value, (8, width))
    for first in range(0, order, step):
        home, base = first // 8, first % 8
        panel = tiles[home]
        entry = {}
        for i in range(step):
            for j in range(i, step):
                entry[i, j] = spread(panel[base + i : base + i + 1, first + j : first + j + 1])
        rows = [spread(panel[base + i : base + i + 1, :]) for i in range(step)]
        inverse = []
        done = []
        for i in range(step):
            row = rows[i]
            if i:
                row = jnp.where((lane >= first) & (lane < first + i), 0.0, row)
            factors = []
            for j in range(i):
                factor = entry[j, i] * inverse[j]
                factors.append(factor)
            for j in range(i):
                source = jnp.where(lane == first + j, 1.0, done[j])
                if i - j > 1:
                    source = jnp.where((lane > first + j) & (lane < first + i), 0.0, source)
                row = row - factors[j] * source
                for m in range(i, step):
                    entry[i, m] = entry[i, m] - factors[j] * entry[j, m]
            inverse.append(1.0 / entry[i, i])
            done.append(row)
        sources = []
        for j in range(step):
            source = jnp.where(lane == first + j, 1.0, done[j])
            if j < step - 1:
                source = jnp.where((lane > first + j) & (lane < first + step), 0.0, source)
            sources.append(source)
        inside = (lane >= first) & (lane < first + step)
        for t in range(home, order // 8):
            if t == home and base + step == 8:
                fresh = tiles[t]
            else:
                columns = [spread(tiles[t][:, first + j : first + j + 1]) for j in range(step)]
                fresh = jnp.where(inside, 0.0, tiles[t])
                for j in range(step):
                    factor = columns[j] * inverse[j]
                    fresh = fresh - factor * sources[j]
                    for m in range(j + 1, step):
                        columns[m] = columns[m] - factor * entry[j, m]
            if t == home:
                fresh = jnp.where(sub < base + step, tiles[t], fresh)
                for j in range(step):
                    fresh = jnp.where(sub == base + j, done[j], fresh)
            tiles[t] = fresh
    return tiles


def finish_kernel(*refs, count, step):
    own_ref, other_ref, high_ref, low_ref, upper_ref, out_ref, staged, sems = refs
    order = upper_ref.shape[0]
    points = high_ref.shape[0] // order
    even = jnp.broadcast_to(lax.rem(lax.axis_index("gz"), 2), (TILE, order)) == 0
    halves = [[], []]
    for r in range(0, order // 2, TILE):
        own, other = own_ref[r : r + TILE, :] / count, other_ref[r : r + TILE, :] / count
        halves[0].append(jnp.where(even, own, other))
        halves[1].append(jnp.where(even, other, own))
    tiles = eliminate(halves[0] + halves[1], order, step)
    lane = lax.broadcasted_iota(jnp.int32, (8, order), 1)
    sub = lax.broadcasted_iota(jnp.int32, (8, order), 0)
    inverse = []
    for t in range(order // 8):
        row = sub + 8 * t
        pivot = jnp.sum(jnp.where(lane == row, tiles[t], 0.0), axis=1, keepdims=True)
        scale = 1.0 / jnp.sqrt(pivot)
        upper_ref[8 * t : 8 * t + 8, :] = jnp.where(lane >= row, tiles[t] * scale, 0.0)
        inverse.append(jnp.where(lane < row, tiles[t], jnp.where(lane == row, 1.0, 0.0)) * scale)
    inverse = jnp.concatenate(inverse, axis=0)
    cols = high_ref.shape[1]
    inverse_parts = two_parts(inverse)
    chunk = points // sems.shape[0]
    copies = []
    for i in range(0, points, 2):
        start = i * order
        wide = [
            jnp.concatenate([ref[start : start + order, :], ref[start + order : start + 2 * order, :]], axis=1)
            for ref in (high_ref, low_ref)
        ]
        out = product(inverse_parts, wide)
        staged[pl.ds(i, order, stride=points), :] = out[:, :cols]
        staged[pl.ds(i + 1, order, stride=points), :] = out[:, cols:]
        if (i + 2) % chunk == 0:
            part = pl.ds(i + 2 - chunk, chunk)
            source = staged.reshape(order, points, cols).at[:, part, :]
            copies.append(pltpu.make_async_copy(source, out_ref.at[:, part, :], sems.at[i // chunk]))
            copies[-1].start()
    for copy in copies:
        copy.wait()


def split_kernel(basis_ref, high_ref, low_ref):
    size = 2 * TILE

    @pl.loop(0, basis_ref.shape[0] // size, unroll=8)
    def _(i):
        here = pl.ds(pl.multiple_of(i * size, size), size)
        high_ref[here, :], low_ref[here, :] = two_parts(basis_ref[here, :])


def two_parts(value):
    high = value.astype(jnp.bfloat16)
    return high, (value - high.astype(jnp.float32)).astype(jnp.bfloat16)


def product(left, right):
    dot = functools.partial(jnp.dot, preferred_element_type=jnp.float32)
    return dot(left[0], right[0]) + (dot(left[0], right[1]) + dot(left[1], right[0]))


def summed(value, rounds_of):
    axes = ("gx", "gy", "gz")
    sizes = [lax.axis_size(name) for name in axes]
    assert all(size & (size - 1) == 0 for size in sizes)

    def index(place):
        return (place[0] * sizes[1] + place[1]) * sizes[2] + place[2]

    for r in range(len(rounds_of[0])):
        got = []
        for chosen in range(1, 1 << len(rounds_of[0][r])):
            pairs = []
            for x in range(sizes[0]):
                for y in range(sizes[1]):
                    for z in range(sizes[2]):
                        partner = [x, y, z]
                        for bit, (axis, mask) in enumerate(rounds_of[z % 2][r]):
                            if chosen >> bit & 1:
                                partner[axes.index(axis)] ^= mask
                        pairs.append((index((x, y, z)), index(partner)))
            got.append(lax.ppermute(value, axes, pairs))
        value = value + got[0]
        if len(got) == 3:
            value = value + (got[1] + got[2])
    return value


def swapped(value, axis, phase):
    pairs = []
    for i in range(phase, lax.axis_size(axis) - 1, 2):
        pairs += [(i, i + 1), (i + 1, i)]
    paired = {i for i, _ in pairs}
    pairs += [(i, i) for i in range(lax.axis_size(axis)) if i not in paired]
    return lax.ppermute(value, axis, pairs)


def sent(value, steps):
    axes = tuple(steps)
    sizes = [lax.axis_size(name) for name in axes]
    pairs = []
    if len(axes) == 1:
        pairs = [(i, i + steps[axes[0]]) for i in range(sizes[0]) if 0 <= i + steps[axes[0]] < sizes[0]]
        return lax.ppermute(value, axes[0], pairs)
    for i in range(sizes[0]):
        for j in range(sizes[1]):
            m, n = i + steps[axes[0]], j + steps[axes[1]]
            if 0 <= m < sizes[0] and 0 <= n < sizes[1]:
                pairs.append((i * sizes[1] + j, m * sizes[1] + n))
    return lax.ppermute(value, axes, pairs)


def local(load_currents, cond_rows, cond_cols, cond_vias, ground, via_offset):
    fields, layers, rows, cols = load_currents.shape
    depth = POWERS
    assert layers == depth and rows == 2 * depth and cols == 4 * depth * rows and fields % TILE == 0
    float_of = lambda *shape: jax.ShapeDtypeStruct(shape, jnp.float32)
    pair = lax.axis_size("gy") == 2
    planes = fields + TILE
    slabs = layers * rows
    high = layers + 2 * depth
    tall = rows + 2 * depth
    count = len(CORNERS)
    part = float_of(slabs // 2, planes, cols)
    flat_rows = (slabs // 2) * (fields + COEFS)
    corner_rows = 2 * count * (fields + COEFS) + slabs * COEFS
    raw = load_currents.reshape(fields * slabs, cols)
    one = swapped(raw, "gz", 0)
    two = swapped(raw, "gz", 1)
    first, second, coef_tiles, coef_rows, shifts = pl.pallas_call(
        edges_kernel,
        out_shape=(
            float_of(flat_rows, cols),
            float_of(flat_rows, cols),
            float_of(slabs, TILE, cols),
            float_of(slabs * COEFS, cols),
            jax.ShapeDtypeStruct((high, TILE, cols), jnp.int32),
        ),
        in_specs=[HBM] * 5 + [SMEM],
        out_specs=(VMEM,) * 5,
        scratch_shapes=[
            pltpu.VMEM((fields * slabs, cols), jnp.float32),
            pltpu.VMEM((COEFS, layers, rows, cols), jnp.float32),
            pltpu.SemaphoreType.DMA((COEFS + 1,)),
        ],
        compiler_params=FIRST,
        name="edges",
    )(raw, cond_rows, cond_cols, cond_vias, ground, via_offset)
    first, second = swapped(first, "gx", 0), swapped(second, "gx", 1)
    block = pl.pallas_call(
        own_kernel,
        out_shape=float_of(slabs, planes, cols),
        in_specs=[VMEM] * 2,
        out_specs=VMEM,
        compiler_params=PARAMS,
        cost_estimate=pl.CostEstimate(flops=0, bytes_accessed=8 * slabs * planes * cols, transcendentals=0),
        name="own",
    )(raw, coef_tiles)
    after, before, to_first, to_second = pl.pallas_call(
        functools.partial(corners_kernel, layers=layers),
        out_shape=(part, part) + (float_of(corner_rows, cols),) * 2,
        in_specs=[VMEM] * 3,
        out_specs=(VMEM,) * 4,
        compiler_params=PARAMS,
        name="corners",
    )(first, second, coef_rows)
    to_first, to_second = swapped(to_first, "gz", 0), swapped(to_second, "gz", 1)
    pieces = (block, after, before, one, two)
    inner = pl.pallas_call(
        functools.partial(inner_kernel, layers=layers, rows=rows),
        out_shape=float_of(high, planes, cols),
        in_specs=[VMEM] * 5,
        out_specs=VMEM,
        compiler_params=PARAMS,
        cost_estimate=pl.CostEstimate(flops=0, bytes_accessed=16 * slabs * planes * cols, transcendentals=0),
        name="inner",
    )(*pieces)
    edge, *outer = pl.pallas_call(
        functools.partial(sides_kernel, layers=layers, rows=rows, pair=pair),
        out_shape=(float_of(high, planes, cols),) + (float_of(high // 2, planes, cols),) * (1 if pair else 2),
        in_specs=[VMEM] * 3,
        out_specs=(VMEM,) * (2 if pair else 3),
        compiler_params=PARAMS,
        name="sides",
    )(inner, to_first, to_second)
    pieces += (to_first, to_second)
    if pair:
        got = [lax.ppermute(outer[0], "gy", [(0, 1), (1, 0)])]
    else:
        got = [sent(outer[0], {"gy": 1}), sent(outer[1], {"gy": -1})]
    start = pl.pallas_call(
        functools.partial(assemble_kernel, layers=layers, rows=rows),
        out_shape=float_of(high, tall, planes, cols),
        in_specs=[VMEM] * 7,
        out_specs=VMEM,
        compiler_params=PARAMS,
        cost_estimate=pl.CostEstimate(flops=0, bytes_accessed=2 * high * tall * planes * cols, transcendentals=0),
        name="assemble",
    )(*pieces)
    order = depth * fields
    points = slabs
    basis, keep, send = pl.pallas_call(
        functools.partial(powers_kernel, fields=fields, layers=layers, rows=rows, pair=pair),
        out_shape=(float_of(points * order, cols),) + (float_of(order // 2, order),) * 2,
        in_specs=[VMEM] * (3 + len(got)),
        out_specs=(VMEM,) * 3,
        scratch_shapes=[
            pltpu.VMEM((depth - 1, high, tall, fields, cols), jnp.float32),
            pltpu.VMEM((7, high, tall, TILE, cols), jnp.float32),
            pltpu.VMEM((2, depth, high, planes, cols), jnp.float32),
            pltpu.VMEM((2, 7, high, TILE, cols), jnp.float32),
            pltpu.VMEM((depth, high, planes, cols), jnp.float32),
            pltpu.VMEM((order, order), jnp.float32),
        ],
        compiler_params=PARAMS,
        name="powers",
    )(start, edge, *got, shifts)
    half_type = jax.ShapeDtypeStruct((points * order, cols), jnp.bfloat16)
    high_part, low_part = pl.pallas_call(
        split_kernel,
        out_shape=(half_type, half_type),
        in_specs=[VMEM],
        out_specs=(VMEM, VMEM),
        compiler_params=PARAMS,
        cost_estimate=pl.CostEstimate(flops=0, bytes_accessed=8 * points * order * cols, transcendentals=0),
        name="split",
    )(basis)
    points_in_all = points * cols
    steps = []
    for axis in ("gx", "gy", "gz"):
        size = lax.axis_size(axis)
        points_in_all *= size
        steps += [(axis, 1 << bit) for bit in range(axis == "gz", size.bit_length() - 1)]
    assert lax.axis_size("gz") % 2 == 0
    across = [(i, i ^ 1) for i in range(lax.axis_size("gz"))]
    own = keep + lax.ppermute(send, "gz", across)
    turns = [steps[i : i + 2] for i in range(0, len(steps), 2)]
    turn = len(turns) // 2 if len(steps) % 2 == 0 else 0
    own = summed(own, (turns, turns[turn:] + turns[:turn]))
    other = lax.ppermute(own, "gz", across)
    upper, basis_q = pl.pallas_call(
        functools.partial(finish_kernel, count=float(points_in_all), step=8),
        out_shape=(float_of(order, order), float_of(order, points, cols)),
        in_specs=[VMEM] * 4,
        out_specs=(VMEM, HBM),
        scratch_shapes=[pltpu.VMEM((order * points, cols), jnp.float32), pltpu.SemaphoreType.DMA((layers,))],
        compiler_params=PARAMS,
        name="finish",
    )(own, other, high_part, low_part)
    return basis_q.reshape(order, layers, rows, cols), upper


def solution(mesh):
    in_specs = (
        P(None, "gz", "gx", "gy"),
        P("gz", "gx", "gy"),
        P("gz", "gx", "gy"),
        P("gz", "gx", "gy"),
        P("gz", "gx", "gy"),
        P(),
    )
    out_specs = (P(None, "gz", "gx", "gy"), P())
    return jax.shard_map(local, mesh=mesh, in_specs=in_specs, out_specs=out_specs, check_vma=False)
```

profile of v0, /device:TPU:0, one launch (start us, length us, event | category | flops | bytes accessed | tf_op | source)
XLA Modules:
  0.0 59.4 jit_solution(3311296522013745353)
XLA Ops:
  0.6 2.8 %edges.1 = (f32[448,128]{1,0:T(8,128)}, f32[448,128]{1,0:T(8,128)}, f32[32,8,128]{2,1,0:T(8,128)}, f32[128,128]{1,0:T(8,128)}, s32[12,8,128]{2,1,0:T(8,128)}) custom-call(f32[768,128]{1,0:T(8,128)} %bitcast.2, f32[4,8,128]{2,1,0:T(8,128)} %rows_ref.1, f32[4,8,128]{2,1,0:T(8,128)} %cols_ref.1, f32[4,8,128]{2,1,0:T(8,128)} %vias_ref.1, ...), custom_call_target="tpu_custom_call" | custom-call | tf_op jit(solution)/shard_map/edges/pallas_call | solution.py:652
  3.4 3.1 %collective-permute-start = (f32[448,128]{1,0:T(8,128)}, f32[448,128]{1,0:T(8,128)S(1)}, u32[]{:S(2)}, u32[]{:S(2)}) collective-permute-start(f32[448,128]{1,0:T(8,128)} %get-tuple-element.21), channel_id=1, source_target_pairs={{0,8},{8,0},{16,24},{24,16},{1,9},{9,1},{17,25},{25,17},{2,10},{10... | collective-permute-start | bytes 688136 | tf_op jit(solution)/shard_map/ppermute | solution.py:617
  6.5 1.6 %collective-permute-start.1 = (f32[448,128]{1,0:T(8,128)}, f32[448,128]{1,0:T(8,128)S(1)}, u32[]{:S(2)}, u32[]{:S(2)}) collective-permute-start(f32[448,128]{1,0:T(8,128)} %get-tuple-element.22), channel_id=1, source_target_pairs={{8,16},{16,8},{0,0},{24,24},{9,17},{17,9},{1,1},{25,25},{10,18},{1... | collective-permute-start | bytes 688136 | tf_op jit(solution)/shard_map/ppermute | solution.py:617
  8.1 1.6 %collective-permute-start.3 = (f32[768,128]{1,0:T(8,128)}, f32[768,128]{1,0:T(8,128)S(1)}, u32[]{:S(2)}, u32[]{:S(2)}) collective-permute-start(f32[768,128]{1,0:T(8,128)} %bitcast.4), channel_id=1, source_target_pairs={{1,2},{2,1},{0,0},{3,3},{5,6},{6,5},{4,4},{7,7},{9,10},{10,9},{8,8... | collective-permute-start | bytes 1179656 | tf_op jit(solution)/shard_map/ppermute | solution.py:617
  9.8 2.6 %collective-permute-done.first_ref = f32[448,128]{1,0:T(8,128)S(1)} collective-permute-done((f32[448,128]{1,0:T(8,128)}, f32[448,128]{1,0:T(8,128)S(1)}, u32[]{:S(2)}, u32[]{:S(2)}) %collective-permute-start) | collective-permute-done | bytes 229408 | tf_op jit(solution)/shard_map/ppermute | solution.py:617
  12.3 0.8 %copy-done.2 = f32[128,128]{1,0:T(8,128)S(1)} copy-done((f32[128,128]{1,0:T(8,128)S(1)}, f32[128,128]{1,0:T(8,128)}, u32[]{:S(2)}) %copy-start.2) | copy-done | bytes 65560
  13.2 0.1 corners.1
  13.4 0.7 %collective-permute-start.5 = (f32[464,128]{1,0:T(8,128)S(1)}, f32[464,128]{1,0:T(8,128)S(1)}, u32[]{:S(2)}, u32[]{:S(2)}) collective-permute-start(f32[464,128]{1,0:T(8,128)S(1)} %get-tuple-element.27), channel_id=1, source_target_pairs={{1,2},{2,1},{0,0},{3,3},{5,6},{6,5},{4,4},{7,7},{9,10},{10,9},{8,8... | collective-permute-start | bytes 712712 | tf_op jit(solution)/shard_map/ppermute | solution.py:617
  14.1 1.0 %copy-done = f32[24,4,8,128]{3,2,1,0:T(8,128)S(1)} copy-done((f32[24,4,8,128]{3,2,1,0:T(8,128)S(1)}, f32[24,4,8,128]{3,2,1,0:T(8,128)}, u32[]{:S(2)}) %copy-start) | copy-done | bytes 393240
  15.0 0.9 %copy-done.1 = f32[32,8,128]{2,1,0:T(8,128)S(1)} copy-done((f32[32,8,128]{2,1,0:T(8,128)S(1)}, f32[32,8,128]{2,1,0:T(8,128)}, u32[]{:S(2)}) %copy-start.1) | copy-done | bytes 131096
  16.0 0.2 own.1.refs_0_
  16.2 1.2 %inner.1.inner_ref = f32[12,32,128]{2,1,0:T(8,128)S(1)} custom-call(f32[32,32,128]{2,1,0:T(8,128)S(1)} %own.1.refs_0_, f32[16,32,128]{2,1,0:T(8,128)S(1)} %get-tuple-element.24.refs_1_, f32[16,32,128]{2,1,0:T(8,128)S(1)} %get-tuple-element.25.refs_2_, f32[768,128]{1,0:T(8,128)S(1)} %collective-permute-done.2.refs_3_, ...), custom_call_target="tpu_custom_call" | custom-call | bytes 2097152 | tf_op jit(solution)/shard_map/inner/pallas_call | solution.py:691
  17.4 0.5 sides.1
  17.9 1.7 %collective-permute-start.6 = (f32[6,32,128]{2,1,0:T(8,128)S(1)}, f32[6,32,128]{2,1,0:T(8,128)S(1)}, u32[]{:S(2)}, u32[]{:S(2)}) collective-permute-start(f32[6,32,128]{2,1,0:T(8,128)S(1)} %get-tuple-element.29), channel_id=1, source_target_pairs={{0,4},{4,0},{1,5},{5,1},{2,6},{6,2},{3,7},{7,3},{8,12},{12,8},{9,1... | collective-permute-start | bytes 294920 | tf_op jit(solution)/shard_map/ppermute | solution.py:710
  19.6 1.1 %assemble.1.refs_0_ = f32[12,16,32,128]{3,2,1,0:T(8,128)S(1)} custom-call(f32[32,32,128]{2,1,0:T(8,128)S(1)} %own.1.refs_0_, f32[16,32,128]{2,1,0:T(8,128)S(1)} %get-tuple-element.24.refs_1_, f32[16,32,128]{2,1,0:T(8,128)S(1)} %get-tuple-element.25.refs_2_, f32[768,128]{1,0:T(8,128)S(1)} %collective-permute-done.2.refs_3_, ...), custom_call_target="tpu_custom_call" | custom-call | bytes 1572864 | tf_op jit(solution)/shard_map/assemble/pallas_call | solution.py:713
  20.7 1.9 %collective-permute-done.6.refs_2_ = f32[6,32,128]{2,1,0:T(8,128)S(1)} collective-permute-done((f32[6,32,128]{2,1,0:T(8,128)S(1)}, f32[6,32,128]{2,1,0:T(8,128)S(1)}, u32[]{:S(2)}, u32[]{:S(2)}) %collective-permute-start.6) | collective-permute-done | bytes 98336 | tf_op jit(solution)/shard_map/ppermute | solution.py:710
  22.6 7.0 %powers.1 = (f32[3072,128]{1,0:T(8,128)S(1)}, f32[48,96]{1,0:T(8,128)S(1)}, f32[48,96]{1,0:T(8,128)S(1)}) custom-call(f32[12,16,32,128]{3,2,1,0:T(8,128)S(1)} %assemble.1.refs_0_, f32[12,32,128]{2,1,0:T(8,128)S(1)} %get-tuple-element.28.refs_1_, f32[6,32,128]{2,1,0:T(8,128)S(1)} %collective-permute-done.6.refs_2_, s32[12,8,128]{2,1,0:T(8,128)S(1)} %copy-done.3), custom_call_target="tpu_custom_call" | custom-call | tf_op jit(solution)/shard_map/powers/pallas_call | solution.py:724
  29.5 2.8 %collective-permute-start.7 = (f32[48,96]{1,0:T(8,128)S(1)}, f32[48,96]{1,0:T(8,128)S(1)}, u32[]{:S(2)}, u32[]{:S(2)}) collective-permute-start(f32[48,96]{1,0:T(8,128)S(1)} %get-tuple-element.32), channel_id=1, source_target_pairs={{0,1},{1,0},{2,3},{3,2},{4,5},{5,4},{6,7},{7,6},{8,9},{9,8},{10,11... | collective-permute-start | bytes 55304 | tf_op jit(solution)/shard_map/ppermute | solution.py:758
  32.3 0.8 %collective-permute-done.7 = f32[48,96]{1,0:T(8,128)S(1)} collective-permute-done((f32[48,96]{1,0:T(8,128)S(1)}, f32[48,96]{1,0:T(8,128)S(1)}, u32[]{:S(2)}, u32[]{:S(2)}) %collective-permute-start.7) | collective-permute-done | bytes 18464 | tf_op jit(solution)/shard_map/ppermute | solution.py:758
  33.2 5.9 %collective-permute-start.9 = (f32[48,96]{1,0:T(8,128)S(1)}, f32[48,96]{1,0:T(8,128)S(1)}, u32[]{:S(2)}, u32[]{:S(2)}) collective-permute-start(f32[48,96]{1,0:T(8,128)S(1)} %add.21), channel_id=1, source_target_pairs={{0,16},{1,3},{2,18},{3,1},{4,20},{5,7},{6,22},{7,5},{8,24},{9,11},... | collective-permute-start | bytes 55304 | tf_op jit(solution)/shard_map/ppermute | solution.py:604
  39.1 1.2 %collective-permute-start.10 = (f32[48,96]{1,0:T(8,128)S(1)}, f32[48,96]{1,0:T(8,128)S(1)}, u32[]{:S(2)}, u32[]{:S(2)}) collective-permute-start(f32[48,96]{1,0:T(8,128)S(1)} %add.21), channel_id=1, source_target_pairs={{0,24},{1,7},{2,26},{3,5},{4,28},{5,3},{6,30},{7,1},{8,16},{9,15},... | collective-permute-start | bytes 55304 | tf_op jit(solution)/shard_map/ppermute | solution.py:604
  40.3 0.6 %collective-permute-done.9 = f32[48,96]{1,0:T(8,128)S(1)} collective-permute-done((f32[48,96]{1,0:T(8,128)S(1)}, f32[48,96]{1,0:T(8,128)S(1)}, u32[]{:S(2)}, u32[]{:S(2)}) %collective-permute-start.9) | collective-permute-done | bytes 18464 | tf_op jit(solution)/shard_map/ppermute | solution.py:604
  40.9 3.8 %collective-permute-done.10 = f32[48,96]{1,0:T(8,128)S(1)} collective-permute-done((f32[48,96]{1,0:T(8,128)S(1)}, f32[48,96]{1,0:T(8,128)S(1)}, u32[]{:S(2)}, u32[]{:S(2)}) %collective-permute-start.10) | collective-permute-done | bytes 18464 | tf_op jit(solution)/shard_map/ppermute | solution.py:604
  44.7 2.6 %collective-permute-start.12 = (f32[48,96]{1,0:T(8,128)S(1)}, f32[48,96]{1,0:T(8,128)S(1)}, u32[]{:S(2)}, u32[]{:S(2)}) collective-permute-start(f32[48,96]{1,0:T(8,128)S(1)} %add_add_fusion.1), channel_id=1, source_target_pairs={{0,2},{1,17},{2,0},{3,19},{4,6},{5,21},{6,4},{7,23},{8,10},{9,25},... | collective-permute-start | bytes 55304 | tf_op jit(solution)/shard_map/ppermute | solution.py:604
  47.3 1.0 %collective-permute-start.13 = (f32[48,96]{1,0:T(8,128)S(1)}, f32[48,96]{1,0:T(8,128)S(1)}, u32[]{:S(2)}, u32[]{:S(2)}) collective-permute-start(f32[48,96]{1,0:T(8,128)S(1)} %add_add_fusion.1), channel_id=1, source_target_pairs={{0,6},{1,25},{2,4},{3,27},{4,2},{5,29},{6,0},{7,31},{8,14},{9,17},... | collective-permute-start | bytes 55304 | tf_op jit(solution)/shard_map/ppermute | solution.py:604
  48.4 0.5 collective-permute-start.11
  48.9 0.3 collective-permute-done.12
  49.1 2.9 %collective-permute-done.13 = f32[48,96]{1,0:T(8,128)S(1)} collective-permute-done((f32[48,96]{1,0:T(8,128)S(1)}, f32[48,96]{1,0:T(8,128)S(1)}, u32[]{:S(2)}, u32[]{:S(2)}) %collective-permute-start.13) | collective-permute-done | bytes 18464 | tf_op jit(solution)/shard_map/ppermute | solution.py:604
  52.1 0.1 collective-permute-done.11
  52.3 0.4 split.1
  52.6 0.8 %collective-permute-done.14.refs_1_ = f32[48,96]{1,0:T(8,128)S(1)} collective-permute-done((f32[48,96]{1,0:T(8,128)S(1)}, f32[48,96]{1,0:T(8,128)S(1)}, u32[]{:S(2)}, u32[]{:S(2)}) %collective-permute-start.14) | collective-permute-done | bytes 18464 | tf_op jit(solution)/shard_map/ppermute | solution.py:762
  53.5 5.8 %finish.1 = (f32[96,96]{1,0:T(8,128)}, f32[96,32,128]{2,1,0:T(8,128)}) custom-call(f32[48,96]{1,0:T(8,128)S(1)} %add_add_fusion.refs_0_, f32[48,96]{1,0:T(8,128)S(1)} %collective-permute-done.14.refs_1_, bf16[3072,128]{1,0:T(8,128)(2,1)S(1)} %get-tuple-element.34.refs_2_, bf16[3072,128]{1,0:T(8,128)(2,1)S(1)} %get-tuple-element.35.refs_3_), custom_call_target="tpu_custom_call" | custom-call | tf_op jit(solution)/shard_map/finish/pallas_call | solution.py:763
  (18 shorter events, 0.2 us)
Async XLA Ops:
  3.4 8.9 %collective-permute-start = (f32[448,128]{1,0:T(8,128)}, f32[448,128]{1,0:T(8,128)S(1)}, u32[]{:S(2)}, u32[]{:S(2)}) collective-permute-start(f32[448,128]{1,0:T(8,128)} %get-tuple-element.21), channel_id=1, source_target_pairs={{0,8},{8,0},{16,24},{24,16},{1,9},{9,1},{17,25},{25,17},{2,10},{10... | collective-permute-start | bytes 688136 | tf_op jit(solution)/shard_map/ppermute | solution.py:617
  6.5 5.8 %collective-permute-start.1 = (f32[448,128]{1,0:T(8,128)}, f32[448,128]{1,0:T(8,128)S(1)}, u32[]{:S(2)}, u32[]{:S(2)}) collective-permute-start(f32[448,128]{1,0:T(8,128)} %get-tuple-element.22), channel_id=1, source_target_pairs={{8,16},{16,8},{0,0},{24,24},{9,17},{17,9},{1,1},{25,25},{10,18},{1... | collective-permute-start | bytes 688136 | tf_op jit(solution)/shard_map/ppermute | solution.py:617
  8.1 8.1 %collective-permute-start.2 = (f32[768,128]{1,0:T(8,128)}, f32[768,128]{1,0:T(8,128)S(1)}, u32[]{:S(2)}, u32[]{:S(2)}) collective-permute-start(f32[768,128]{1,0:T(8,128)} %bitcast.3), channel_id=1, source_target_pairs={{0,1},{1,0},{2,3},{3,2},{4,5},{5,4},{6,7},{7,6},{8,9},{9,8},{10,11... | collective-permute-start | bytes 1179656 | tf_op jit(solution)/shard_map/ppermute | solution.py:617
  8.1 8.1 %collective-permute-start.3 = (f32[768,128]{1,0:T(8,128)}, f32[768,128]{1,0:T(8,128)S(1)}, u32[]{:S(2)}, u32[]{:S(2)}) collective-permute-start(f32[768,128]{1,0:T(8,128)} %bitcast.4), channel_id=1, source_target_pairs={{1,2},{2,1},{0,0},{3,3},{5,6},{6,5},{4,4},{7,7},{9,10},{10,9},{8,8... | collective-permute-start | bytes 1179656 | tf_op jit(solution)/shard_map/ppermute | solution.py:617
  12.3 0.8 %copy-start.2 = (f32[128,128]{1,0:T(8,128)S(1)}, f32[128,128]{1,0:T(8,128)}, u32[]{:S(2)}) copy-start(f32[128,128]{1,0:T(8,128)} %get-tuple-element.23.flat_ref) | copy-start | bytes 196612
  13.3 4.1 %collective-permute-start.4 = (f32[464,128]{1,0:T(8,128)S(1)}, f32[464,128]{1,0:T(8,128)S(1)}, u32[]{:S(2)}, u32[]{:S(2)}) collective-permute-start(f32[464,128]{1,0:T(8,128)S(1)} %get-tuple-element.26), channel_id=1, source_target_pairs={{0,1},{1,0},{2,3},{3,2},{4,5},{5,4},{6,7},{7,6},{8,9},{9,8},{10,11... | collective-permute-start | bytes 712712 | tf_op jit(solution)/shard_map/ppermute | solution.py:617
  13.4 4.0 %collective-permute-start.5 = (f32[464,128]{1,0:T(8,128)S(1)}, f32[464,128]{1,0:T(8,128)S(1)}, u32[]{:S(2)}, u32[]{:S(2)}) collective-permute-start(f32[464,128]{1,0:T(8,128)S(1)} %get-tuple-element.27), channel_id=1, source_target_pairs={{1,2},{2,1},{0,0},{3,3},{5,6},{6,5},{4,4},{7,7},{9,10},{10,9},{8,8... | collective-permute-start | bytes 712712 | tf_op jit(solution)/shard_map/ppermute | solution.py:617
  14.0 1.0 %copy-start = (f32[24,4,8,128]{3,2,1,0:T(8,128)S(1)}, f32[24,4,8,128]{3,2,1,0:T(8,128)}, u32[]{:S(2)}) copy-start(f32[24,4,8,128]{3,2,1,0:T(8,128)} %param.6) | copy-start | bytes 1179652
  15.0 0.9 %copy-start.1 = (f32[32,8,128]{2,1,0:T(8,128)S(1)}, f32[32,8,128]{2,1,0:T(8,128)}, u32[]{:S(2)}) copy-start(f32[32,8,128]{2,1,0:T(8,128)} %get-tuple-element.20.tile_ref) | copy-start | bytes 393220
  17.9 4.7 %copy-start.3 = (s32[12,8,128]{2,1,0:T(8,128)S(1)}, s32[12,8,128]{2,1,0:T(8,128)}, u32[]{:S(2)}) copy-start(s32[12,8,128]{2,1,0:T(8,128)} %get-tuple-element.30.refs_3_) | copy-start | bytes 147460
  17.9 4.7 %collective-permute-start.6 = (f32[6,32,128]{2,1,0:T(8,128)S(1)}, f32[6,32,128]{2,1,0:T(8,128)S(1)}, u32[]{:S(2)}, u32[]{:S(2)}) collective-permute-start(f32[6,32,128]{2,1,0:T(8,128)S(1)} %get-tuple-element.29), channel_id=1, source_target_pairs={{0,4},{4,0},{1,5},{5,1},{2,6},{6,2},{3,7},{7,3},{8,12},{12,8},{9,1... | collective-permute-start | bytes 294920 | tf_op jit(solution)/shard_map/ppermute | solution.py:710
  29.5 3.6 %collective-permute-start.7 = (f32[48,96]{1,0:T(8,128)S(1)}, f32[48,96]{1,0:T(8,128)S(1)}, u32[]{:S(2)}, u32[]{:S(2)}) collective-permute-start(f32[48,96]{1,0:T(8,128)S(1)} %get-tuple-element.32), channel_id=1, source_target_pairs={{0,1},{1,0},{2,3},{3,2},{4,5},{5,4},{6,7},{7,6},{8,9},{9,8},{10,11... | collective-permute-start | bytes 55304 | tf_op jit(solution)/shard_map/ppermute | solution.py:758
  33.2 7.7 %collective-permute-start.9 = (f32[48,96]{1,0:T(8,128)S(1)}, f32[48,96]{1,0:T(8,128)S(1)}, u32[]{:S(2)}, u32[]{:S(2)}) collective-permute-start(f32[48,96]{1,0:T(8,128)S(1)} %add.21), channel_id=1, source_target_pairs={{0,16},{1,3},{2,18},{3,1},{4,20},{5,7},{6,22},{7,5},{8,24},{9,11},... | collective-permute-start | bytes 55304 | tf_op jit(solution)/shard_map/ppermute | solution.py:604
  39.1 5.6 %collective-permute-start.10 = (f32[48,96]{1,0:T(8,128)S(1)}, f32[48,96]{1,0:T(8,128)S(1)}, u32[]{:S(2)}, u32[]{:S(2)}) collective-permute-start(f32[48,96]{1,0:T(8,128)S(1)} %add.21), channel_id=1, source_target_pairs={{0,24},{1,7},{2,26},{3,5},{4,28},{5,3},{6,30},{7,1},{8,16},{9,15},... | collective-permute-start | bytes 55304 | tf_op jit(solution)/shard_map/ppermute | solution.py:604
  40.3 4.4 %collective-permute-start.8 = (f32[48,96]{1,0:T(8,128)S(1)}, f32[48,96]{1,0:T(8,128)S(1)}, u32[]{:S(2)}, u32[]{:S(2)}) collective-permute-start(f32[48,96]{1,0:T(8,128)S(1)} %add.21), channel_id=1, source_target_pairs={{0,8},{1,5},{2,10},{3,7},{4,12},{5,1},{6,14},{7,3},{8,0},{9,13},{1... | collective-permute-start | bytes 55304 | tf_op jit(solution)/shard_map/ppermute | solution.py:604
  44.7 4.4 %collective-permute-start.12 = (f32[48,96]{1,0:T(8,128)S(1)}, f32[48,96]{1,0:T(8,128)S(1)}, u32[]{:S(2)}, u32[]{:S(2)}) collective-permute-start(f32[48,96]{1,0:T(8,128)S(1)} %add_add_fusion.1), channel_id=1, source_target_pairs={{0,2},{1,17},{2,0},{3,19},{4,6},{5,21},{6,4},{7,23},{8,10},{9,25},... | collective-permute-start | bytes 55304 | tf_op jit(solution)/shard_map/ppermute | solution.py:604
  47.3 4.7 %collective-permute-start.13 = (f32[48,96]{1,0:T(8,128)S(1)}, f32[48,96]{1,0:T(8,128)S(1)}, u32[]{:S(2)}, u32[]{:S(2)}) collective-permute-start(f32[48,96]{1,0:T(8,128)S(1)} %add_add_fusion.1), channel_id=1, source_target_pairs={{0,6},{1,25},{2,4},{3,27},{4,2},{5,29},{6,0},{7,31},{8,14},{9,17},... | collective-permute-start | bytes 55304 | tf_op jit(solution)/shard_map/ppermute | solution.py:604
  48.4 3.8 %collective-permute-start.11 = (f32[48,96]{1,0:T(8,128)S(1)}, f32[48,96]{1,0:T(8,128)S(1)}, u32[]{:S(2)}, u32[]{:S(2)}) collective-permute-start(f32[48,96]{1,0:T(8,128)S(1)} %add_add_fusion.1), channel_id=1, source_target_pairs={{0,4},{1,9},{2,6},{3,11},{4,0},{5,13},{6,2},{7,15},{8,12},{9,1},{1... | collective-permute-start | bytes 55304 | tf_op jit(solution)/shard_map/ppermute | solution.py:604
  52.2 1.3 %collective-permute-start.14 = (f32[48,96]{1,0:T(8,128)S(1)}, f32[48,96]{1,0:T(8,128)S(1)}, u32[]{:S(2)}, u32[]{:S(2)}) collective-permute-start(f32[48,96]{1,0:T(8,128)S(1)} %add_add_fusion.refs_0_), channel_id=1, source_target_pairs={{0,1},{1,0},{2,3},{3,2},{4,5},{5,4},{6,7},{7,6},{8,9},{9,8},{10,11... | collective-permute-start | bytes 55304 | tf_op jit(solution)/shard_map/ppermute | solution.py:762
where the time goes:
time: 59.7 us; the launch traced here: 59.4 us
  starting transfers between devices  22.9 us (38%)
  Pallas kernels  18.9 us (32%)
  waiting for transfers between devices  13.9 us (23%)
  local copies, waits for them, and re-layouts  2.74 us (5%)
  between operations  0.91 us (2%)
    ppermute x6, starting transfers between devices, summed(): got.append(lax.ppermute(value, axes, pairs))  11.3 us
    ppermute x6, waiting for transfers between devices, summed(): got.append(lax.ppermute(value, axes, pairs))  7.73 us
    ppermute x6, starting transfers between devices, swapped(): return lax.ppermute(value, axis, pairs)  7.07 us
    pallas_call x1, Pallas kernels, local(): pl.pallas_call(functools.partial(powers_kernel, fields=fields, layers=lay...  6.95 us
    pallas_call x1, Pallas kernels, local(): pl.pallas_call(functools.partial(finish_kernel, count=float(points_in_all...  5.77 us
    ppermute x1, starting transfers between devices, local(): own = keep + lax.ppermute(send, 'gz', across)  2.8 us
    pallas_call x1, Pallas kernels, local(): pl.pallas_call(edges_kernel, out_shape=(float_of(flat_rows, cols), float_...  2.8 us
    unnamed x8, local copies, waits for them, and re-layouts  2.74 us
  transfers between devices with their start and end apart: 15, of which 9 were waited for; matrix products, arithmetic and copies ran while one was open for 0% of the time, Pallas kernels for 5%

commit v1 on v0

--- a/solution.py
+++ b/solution.py
@@ -310,14 +310,7 @@
     thetas = [shift * basis_scale for shift in newton_shifts]
 
     early = lax.rem(lane, group) < depth
-    if pair:
-        first_side = jnp.where(gy == 0, 1, 0)
-        last_side = first_side + 1
-    else:
-        first_side, last_side = 0, 2
-
-    @pl.loop(first_side, last_side)
-    def _(side):
+    def advance_strip(side):
         left_side = jnp.broadcast_to(side, (TILE, cols)) == 0
         from_edge = early != left_side
         for e in range(high):
@@ -363,12 +356,16 @@
                         from_below(look(e - 1, f), under),
                     )
 
+    if pair:
+        advance_strip(jnp.where(gy == 0, 1, 0))
+    else:
+        pl.loop(0, 2)(advance_strip)
+
     gy_lane = jnp.broadcast_to(gy, (TILE, cols))
     on_left = (lax.rem(lane, group) == depth - 1) & (gy_lane > 0)
     on_right = (lax.rem(lane, group) == depth - 2) & (gy_lane < lax.axis_size("gy") - 1)
 
-    @pl.loop(0, high)
-    def _(e):
+    for e in range(high):
         for k in range(depth):
             for f in range(0, planes if k == 0 else fields, TILE):
                 here = slice(f, f + TILE)

time: 59.7 us -> 58.7 us (0.983)
  Pallas kernels: 18.9 us -> 18.1 us
    pallas_call x1, Pallas kernels: 6.95 us -> 5.91 us  [local(): pl.pallas_call(functools.partial(powers_kernel, fields=fields, layers=lay...]
where the time goes in v1:
time: 58.7 us; the launch traced here: 58.3 us
  starting transfers between devices  22.9 us (39%)
  Pallas kernels  18.1 us (31%)
  waiting for transfers between devices  13.7 us (23%)
  local copies, waits for them, and re-layouts  2.74 us (5%)
  between operations  0.91 us (2%)
    ppermute x6, starting transfers between devices, summed(): got.append(lax.ppermute(value, axes, pairs))  11.3 us
    ppermute x6, waiting for transfers between devices, summed(): got.append(lax.ppermute(value, axes, pairs))  7.74 us
    ppermute x6, starting transfers between devices, swapped(): return lax.ppermute(value, axis, pairs)  7.07 us
    pallas_call x1, Pallas kernels, local(): pl.pallas_call(functools.partial(powers_kernel, fields=fields, layers=lay...  5.91 us
    pallas_call x1, Pallas kernels, local(): pl.pallas_call(functools.partial(finish_kernel, count=float(points_in_all...  5.77 us
    ppermute x1, starting transfers between devices, local(): own = keep + lax.ppermute(send, 'gz', across)  2.8 us
    pallas_call x1, Pallas kernels, local(): pl.pallas_call(edges_kernel, out_shape=(float_of(flat_rows, cols), float_...  2.8 us
    unnamed x8, local copies, waits for them, and re-layouts  2.74 us
  transfers between devices with their start and end apart: 15, of which 9 were waited for; matrix products, arithmetic and copies ran while one was open for 0% of the time, Pallas kernels for 5%

profile of v1, /device:TPU:0, one launch (start us, length us, event | category | flops | bytes accessed | tf_op | source)
XLA Modules:
  0.0 58.3 jit_solution(15160121802135815014)
XLA Ops:
  0.6 2.8 %edges.1 = (f32[448,128]{1,0:T(8,128)}, f32[448,128]{1,0:T(8,128)}, f32[32,8,128]{2,1,0:T(8,128)}, f32[128,128]{1,0:T(8,128)}, s32[12,8,128]{2,1,0:T(8,128)}) custom-call(f32[768,128]{1,0:T(8,128)} %bitcast.2, f32[4,8,128]{2,1,0:T(8,128)} %rows_ref.1, f32[4,8,128]{2,1,0:T(8,128)} %cols_ref.1, f32[4,8,128]{2,1,0:T(8,128)} %vias_ref.1, ...), custom_call_target="tpu_custom_call" | custom-call | tf_op jit(solution)/shard_map/edges/pallas_call | solution.py:649
  3.4 3.1 %collective-permute-start = (f32[448,128]{1,0:T(8,128)}, f32[448,128]{1,0:T(8,128)S(1)}, u32[]{:S(2)}, u32[]{:S(2)}) collective-permute-start(f32[448,128]{1,0:T(8,128)} %get-tuple-element.21), channel_id=1, source_target_pairs={{0,8},{8,0},{16,24},{24,16},{1,9},{9,1},{17,25},{25,17},{2,10},{10... | collective-permute-start | bytes 688136 | tf_op jit(solution)/shard_map/ppermute | solution.py:614
  6.5 1.6 %collective-permute-start.1 = (f32[448,128]{1,0:T(8,128)}, f32[448,128]{1,0:T(8,128)S(1)}, u32[]{:S(2)}, u32[]{:S(2)}) collective-permute-start(f32[448,128]{1,0:T(8,128)} %get-tuple-element.22), channel_id=1, source_target_pairs={{8,16},{16,8},{0,0},{24,24},{9,17},{17,9},{1,1},{25,25},{10,18},{1... | collective-permute-start | bytes 688136 | tf_op jit(solution)/shard_map/ppermute | solution.py:614
  8.1 1.6 %collective-permute-start.3 = (f32[768,128]{1,0:T(8,128)}, f32[768,128]{1,0:T(8,128)S(1)}, u32[]{:S(2)}, u32[]{:S(2)}) collective-permute-start(f32[768,128]{1,0:T(8,128)} %bitcast.4), channel_id=1, source_target_pairs={{1,2},{2,1},{0,0},{3,3},{5,6},{6,5},{4,4},{7,7},{9,10},{10,9},{8,8... | collective-permute-start | bytes 1179656 | tf_op jit(solution)/shard_map/ppermute | solution.py:614
  9.8 2.6 %collective-permute-done.first_ref = f32[448,128]{1,0:T(8,128)S(1)} collective-permute-done((f32[448,128]{1,0:T(8,128)}, f32[448,128]{1,0:T(8,128)S(1)}, u32[]{:S(2)}, u32[]{:S(2)}) %collective-permute-start) | collective-permute-done | bytes 229408 | tf_op jit(solution)/shard_map/ppermute | solution.py:614
  12.3 0.8 %copy-done.2 = f32[128,128]{1,0:T(8,128)S(1)} copy-done((f32[128,128]{1,0:T(8,128)S(1)}, f32[128,128]{1,0:T(8,128)}, u32[]{:S(2)}) %copy-start.2) | copy-done | bytes 65560
  13.2 0.1 corners.1
  13.4 0.7 %collective-permute-start.5 = (f32[464,128]{1,0:T(8,128)S(1)}, f32[464,128]{1,0:T(8,128)S(1)}, u32[]{:S(2)}, u32[]{:S(2)}) collective-permute-start(f32[464,128]{1,0:T(8,128)S(1)} %get-tuple-element.27), channel_id=1, source_target_pairs={{1,2},{2,1},{0,0},{3,3},{5,6},{6,5},{4,4},{7,7},{9,10},{10,9},{8,8... | collective-permute-start | bytes 712712 | tf_op jit(solution)/shard_map/ppermute | solution.py:614
  14.1 1.0 %copy-done = f32[24,4,8,128]{3,2,1,0:T(8,128)S(1)} copy-done((f32[24,4,8,128]{3,2,1,0:T(8,128)S(1)}, f32[24,4,8,128]{3,2,1,0:T(8,128)}, u32[]{:S(2)}) %copy-start) | copy-done | bytes 393240
  15.0 0.9 %copy-done.1 = f32[32,8,128]{2,1,0:T(8,128)S(1)} copy-done((f32[32,8,128]{2,1,0:T(8,128)S(1)}, f32[32,8,128]{2,1,0:T(8,128)}, u32[]{:S(2)}) %copy-start.1) | copy-done | bytes 131096
  16.0 0.2 own.1.refs_0_
  16.2 1.2 %inner.1.inner_ref = f32[12,32,128]{2,1,0:T(8,128)S(1)} custom-call(f32[32,32,128]{2,1,0:T(8,128)S(1)} %own.1.refs_0_, f32[16,32,128]{2,1,0:T(8,128)S(1)} %get-tuple-element.24.refs_1_, f32[16,32,128]{2,1,0:T(8,128)S(1)} %get-tuple-element.25.refs_2_, f32[768,128]{1,0:T(8,128)S(1)} %collective-permute-done.2.refs_3_, ...), custom_call_target="tpu_custom_call" | custom-call | bytes 2097152 | tf_op jit(solution)/shard_map/inner/pallas_call | solution.py:688
  17.4 0.5 sides.1
  17.9 1.7 %collective-permute-start.6 = (f32[6,32,128]{2,1,0:T(8,128)S(1)}, f32[6,32,128]{2,1,0:T(8,128)S(1)}, u32[]{:S(2)}, u32[]{:S(2)}) collective-permute-start(f32[6,32,128]{2,1,0:T(8,128)S(1)} %get-tuple-element.29), channel_id=1, source_target_pairs={{0,4},{4,0},{1,5},{5,1},{2,6},{6,2},{3,7},{7,3},{8,12},{12,8},{9,1... | collective-permute-start | bytes 294920 | tf_op jit(solution)/shard_map/ppermute | solution.py:707
  19.6 1.1 %assemble.1.refs_0_ = f32[12,16,32,128]{3,2,1,0:T(8,128)S(1)} custom-call(f32[32,32,128]{2,1,0:T(8,128)S(1)} %own.1.refs_0_, f32[16,32,128]{2,1,0:T(8,128)S(1)} %get-tuple-element.24.refs_1_, f32[16,32,128]{2,1,0:T(8,128)S(1)} %get-tuple-element.25.refs_2_, f32[768,128]{1,0:T(8,128)S(1)} %collective-permute-done.2.refs_3_, ...), custom_call_target="tpu_custom_call" | custom-call | bytes 1572864 | tf_op jit(solution)/shard_map/assemble/pallas_call | solution.py:710
  20.7 1.9 %collective-permute-done.6.refs_2_ = f32[6,32,128]{2,1,0:T(8,128)S(1)} collective-permute-done((f32[6,32,128]{2,1,0:T(8,128)S(1)}, f32[6,32,128]{2,1,0:T(8,128)S(1)}, u32[]{:S(2)}, u32[]{:S(2)}) %collective-permute-start.6) | collective-permute-done | bytes 98336 | tf_op jit(solution)/shard_map/ppermute | solution.py:707
  22.6 5.9 %powers.1 = (f32[3072,128]{1,0:T(8,128)S(1)}, f32[48,96]{1,0:T(8,128)S(1)}, f32[48,96]{1,0:T(8,128)S(1)}) custom-call(f32[12,16,32,128]{3,2,1,0:T(8,128)S(1)} %assemble.1.refs_0_, f32[12,32,128]{2,1,0:T(8,128)S(1)} %get-tuple-element.28.refs_1_, f32[6,32,128]{2,1,0:T(8,128)S(1)} %collective-permute-done.6.refs_2_, s32[12,8,128]{2,1,0:T(8,128)S(1)} %copy-done.3), custom_call_target="tpu_custom_call" | custom-call | tf_op jit(solution)/shard_map/powers/pallas_call | solution.py:721
  28.5 2.8 %collective-permute-start.7 = (f32[48,96]{1,0:T(8,128)S(1)}, f32[48,96]{1,0:T(8,128)S(1)}, u32[]{:S(2)}, u32[]{:S(2)}) collective-permute-start(f32[48,96]{1,0:T(8,128)S(1)} %get-tuple-element.32), channel_id=1, source_target_pairs={{0,1},{1,0},{2,3},{3,2},{4,5},{5,4},{6,7},{7,6},{8,9},{9,8},{10,11... | collective-permute-start | bytes 55304 | tf_op jit(solution)/shard_map/ppermute | solution.py:755
  31.3 0.8 %collective-permute-done.7 = f32[48,96]{1,0:T(8,128)S(1)} collective-permute-done((f32[48,96]{1,0:T(8,128)S(1)}, f32[48,96]{1,0:T(8,128)S(1)}, u32[]{:S(2)}, u32[]{:S(2)}) %collective-permute-start.7) | collective-permute-done | bytes 18464 | tf_op jit(solution)/shard_map/ppermute | solution.py:755
  32.1 5.9 %collective-permute-start.9 = (f32[48,96]{1,0:T(8,128)S(1)}, f32[48,96]{1,0:T(8,128)S(1)}, u32[]{:S(2)}, u32[]{:S(2)}) collective-permute-start(f32[48,96]{1,0:T(8,128)S(1)} %add.21), channel_id=1, source_target_pairs={{0,16},{1,3},{2,18},{3,1},{4,20},{5,7},{6,22},{7,5},{8,24},{9,11},... | collective-permute-start | bytes 55304 | tf_op jit(solution)/shard_map/ppermute | solution.py:601
  38.1 1.2 %collective-permute-start.10 = (f32[48,96]{1,0:T(8,128)S(1)}, f32[48,96]{1,0:T(8,128)S(1)}, u32[]{:S(2)}, u32[]{:S(2)}) collective-permute-start(f32[48,96]{1,0:T(8,128)S(1)} %add.21), channel_id=1, source_target_pairs={{0,24},{1,7},{2,26},{3,5},{4,28},{5,3},{6,30},{7,1},{8,16},{9,15},... | collective-permute-start | bytes 55304 | tf_op jit(solution)/shard_map/ppermute | solution.py:601
  39.2 0.6 %collective-permute-done.9 = f32[48,96]{1,0:T(8,128)S(1)} collective-permute-done((f32[48,96]{1,0:T(8,128)S(1)}, f32[48,96]{1,0:T(8,128)S(1)}, u32[]{:S(2)}, u32[]{:S(2)}) %collective-permute-start.9) | collective-permute-done | bytes 18464 | tf_op jit(solution)/shard_map/ppermute | solution.py:601
  39.9 3.8 %collective-permute-done.10 = f32[48,96]{1,0:T(8,128)S(1)} collective-permute-done((f32[48,96]{1,0:T(8,128)S(1)}, f32[48,96]{1,0:T(8,128)S(1)}, u32[]{:S(2)}, u32[]{:S(2)}) %collective-permute-start.10) | collective-permute-done | bytes 18464 | tf_op jit(solution)/shard_map/ppermute | solution.py:601
  43.7 2.6 %collective-permute-start.12 = (f32[48,96]{1,0:T(8,128)S(1)}, f32[48,96]{1,0:T(8,128)S(1)}, u32[]{:S(2)}, u32[]{:S(2)}) collective-permute-start(f32[48,96]{1,0:T(8,128)S(1)} %add_add_fusion.1), channel_id=1, source_target_pairs={{0,2},{1,17},{2,0},{3,19},{4,6},{5,21},{6,4},{7,23},{8,10},{9,25},... | collective-permute-start | bytes 55304 | tf_op jit(solution)/shard_map/ppermute | solution.py:601
  46.3 1.0 %collective-permute-start.13 = (f32[48,96]{1,0:T(8,128)S(1)}, f32[48,96]{1,0:T(8,128)S(1)}, u32[]{:S(2)}, u32[]{:S(2)}) collective-permute-start(f32[48,96]{1,0:T(8,128)S(1)} %add_add_fusion.1), channel_id=1, source_target_pairs={{0,6},{1,25},{2,4},{3,27},{4,2},{5,29},{6,0},{7,31},{8,14},{9,17},... | collective-permute-start | bytes 55304 | tf_op jit(solution)/shard_map/ppermute | solution.py:601
  47.3 0.5 collective-permute-start.11
  47.8 0.3 collective-permute-done.12
  48.1 2.9 %collective-permute-done.13 = f32[48,96]{1,0:T(8,128)S(1)} collective-permute-done((f32[48,96]{1,0:T(8,128)S(1)}, f32[48,96]{1,0:T(8,128)S(1)}, u32[]{:S(2)}, u32[]{:S(2)}) %collective-permute-start.13) | collective-permute-done | bytes 18464 | tf_op jit(solution)/shard_map/ppermute | solution.py:601
  51.0 0.1 collective-permute-done.11
  51.2 0.5 split.1
  51.8 0.6 %collective-permute-done.14.refs_1_ = f32[48,96]{1,0:T(8,128)S(1)} collective-permute-done((f32[48,96]{1,0:T(8,128)S(1)}, f32[48,96]{1,0:T(8,128)S(1)}, u32[]{:S(2)}, u32[]{:S(2)}) %collective-permute-start.14) | collective-permute-done | bytes 18464 | tf_op jit(solution)/shard_map/ppermute | solution.py:759
  52.4 5.8 %finish.1 = (f32[96,96]{1,0:T(8,128)}, f32[96,32,128]{2,1,0:T(8,128)}) custom-call(f32[48,96]{1,0:T(8,128)S(1)} %add_add_fusion.refs_0_, f32[48,96]{1,0:T(8,128)S(1)} %collective-permute-done.14.refs_1_, bf16[3072,128]{1,0:T(8,128)(2,1)S(1)} %get-tuple-element.34.refs_2_, bf16[3072,128]{1,0:T(8,128)(2,1)S(1)} %get-tuple-element.35.refs_3_), custom_call_target="tpu_custom_call" | custom-call | tf_op jit(solution)/shard_map/finish/pallas_call | solution.py:760
  (18 shorter events, 0.2 us)
Async XLA Ops:
  3.4 8.9 %collective-permute-start = (f32[448,128]{1,0:T(8,128)}, f32[448,128]{1,0:T(8,128)S(1)}, u32[]{:S(2)}, u32[]{:S(2)}) collective-permute-start(f32[448,128]{1,0:T(8,128)} %get-tuple-element.21), channel_id=1, source_target_pairs={{0,8},{8,0},{16,24},{24,16},{1,9},{9,1},{17,25},{25,17},{2,10},{10... | collective-permute-start | bytes 688136 | tf_op jit(solution)/shard_map/ppermute | solution.py:614
  6.5 5.8 %collective-permute-start.1 = (f32[448,128]{1,0:T(8,128)}, f32[448,128]{1,0:T(8,128)S(1)}, u32[]{:S(2)}, u32[]{:S(2)}) collective-permute-start(f32[448,128]{1,0:T(8,128)} %get-tuple-element.22), channel_id=1, source_target_pairs={{8,16},{16,8},{0,0},{24,24},{9,17},{17,9},{1,1},{25,25},{10,18},{1... | collective-permute-start | bytes 688136 | tf_op jit(solution)/shard_map/ppermute | solution.py:614
  8.1 8.1 %collective-permute-start.2 = (f32[768,128]{1,0:T(8,128)}, f32[768,128]{1,0:T(8,128)S(1)}, u32[]{:S(2)}, u32[]{:S(2)}) collective-permute-start(f32[768,128]{1,0:T(8,128)} %bitcast.3), channel_id=1, source_target_pairs={{0,1},{1,0},{2,3},{3,2},{4,5},{5,4},{6,7},{7,6},{8,9},{9,8},{10,11... | collective-permute-start | bytes 1179656 | tf_op jit(solution)/shard_map/ppermute | solution.py:614
  8.1 8.1 %collective-permute-start.3 = (f32[768,128]{1,0:T(8,128)}, f32[768,128]{1,0:T(8,128)S(1)}, u32[]{:S(2)}, u32[]{:S(2)}) collective-permute-start(f32[768,128]{1,0:T(8,128)} %bitcast.4), channel_id=1, source_target_pairs={{1,2},{2,1},{0,0},{3,3},{5,6},{6,5},{4,4},{7,7},{9,10},{10,9},{8,8... | collective-permute-start | bytes 1179656 | tf_op jit(solution)/shard_map/ppermute | solution.py:614
  12.3 0.8 %copy-start.2 = (f32[128,128]{1,0:T(8,128)S(1)}, f32[128,128]{1,0:T(8,128)}, u32[]{:S(2)}) copy-start(f32[128,128]{1,0:T(8,128)} %get-tuple-element.23.flat_ref) | copy-start | bytes 196612
  13.3 4.1 %collective-permute-start.4 = (f32[464,128]{1,0:T(8,128)S(1)}, f32[464,128]{1,0:T(8,128)S(1)}, u32[]{:S(2)}, u32[]{:S(2)}) collective-permute-start(f32[464,128]{1,0:T(8,128)S(1)} %get-tuple-element.26), channel_id=1, source_target_pairs={{0,1},{1,0},{2,3},{3,2},{4,5},{5,4},{6,7},{7,6},{8,9},{9,8},{10,11... | collective-permute-start | bytes 712712 | tf_op jit(solution)/shard_map/ppermute | solution.py:614
  13.4 4.0 %collective-permute-start.5 = (f32[464,128]{1,0:T(8,128)S(1)}, f32[464,128]{1,0:T(8,128)S(1)}, u32[]{:S(2)}, u32[]{:S(2)}) collective-permute-start(f32[464,128]{1,0:T(8,128)S(1)} %get-tuple-element.27), channel_id=1, source_target_pairs={{1,2},{2,1},{0,0},{3,3},{5,6},{6,5},{4,4},{7,7},{9,10},{10,9},{8,8... | collective-permute-start | bytes 712712 | tf_op jit(solution)/shard_map/ppermute | solution.py:614
  14.0 1.0 %copy-start = (f32[24,4,8,128]{3,2,1,0:T(8,128)S(1)}, f32[24,4,8,128]{3,2,1,0:T(8,128)}, u32[]{:S(2)}) copy-start(f32[24,4,8,128]{3,2,1,0:T(8,128)} %param.6) | copy-start | bytes 1179652
  15.0 0.9 %copy-start.1 = (f32[32,8,128]{2,1,0:T(8,128)S(1)}, f32[32,8,128]{2,1,0:T(8,128)}, u32[]{:S(2)}) copy-start(f32[32,8,128]{2,1,0:T(8,128)} %get-tuple-element.20.tile_ref) | copy-start | bytes 393220
  17.9 4.7 %copy-start.3 = (s32[12,8,128]{2,1,0:T(8,128)S(1)}, s32[12,8,128]{2,1,0:T(8,128)}, u32[]{:S(2)}) copy-start(s32[12,8,128]{2,1,0:T(8,128)} %get-tuple-element.30.refs_3_) | copy-start | bytes 147460
  17.9 4.7 %collective-permute-start.6 = (f32[6,32,128]{2,1,0:T(8,128)S(1)}, f32[6,32,128]{2,1,0:T(8,128)S(1)}, u32[]{:S(2)}, u32[]{:S(2)}) collective-permute-start(f32[6,32,128]{2,1,0:T(8,128)S(1)} %get-tuple-element.29), channel_id=1, source_target_pairs={{0,4},{4,0},{1,5},{5,1},{2,6},{6,2},{3,7},{7,3},{8,12},{12,8},{9,1... | collective-permute-start | bytes 294920 | tf_op jit(solution)/shard_map/ppermute | solution.py:707
  28.5 3.6 %collective-permute-start.7 = (f32[48,96]{1,0:T(8,128)S(1)}, f32[48,96]{1,0:T(8,128)S(1)}, u32[]{:S(2)}, u32[]{:S(2)}) collective-permute-start(f32[48,96]{1,0:T(8,128)S(1)} %get-tuple-element.32), channel_id=1, source_target_pairs={{0,1},{1,0},{2,3},{3,2},{4,5},{5,4},{6,7},{7,6},{8,9},{9,8},{10,11... | collective-permute-start | bytes 55304 | tf_op jit(solution)/shard_map/ppermute | solution.py:755
  32.1 7.7 %collective-permute-start.9 = (f32[48,96]{1,0:T(8,128)S(1)}, f32[48,96]{1,0:T(8,128)S(1)}, u32[]{:S(2)}, u32[]{:S(2)}) collective-permute-start(f32[48,96]{1,0:T(8,128)S(1)} %add.21), channel_id=1, source_target_pairs={{0,16},{1,3},{2,18},{3,1},{4,20},{5,7},{6,22},{7,5},{8,24},{9,11},... | collective-permute-start | bytes 55304 | tf_op jit(solution)/shard_map/ppermute | solution.py:601
  38.1 5.6 %collective-permute-start.10 = (f32[48,96]{1,0:T(8,128)S(1)}, f32[48,96]{1,0:T(8,128)S(1)}, u32[]{:S(2)}, u32[]{:S(2)}) collective-permute-start(f32[48,96]{1,0:T(8,128)S(1)} %add.21), channel_id=1, source_target_pairs={{0,24},{1,7},{2,26},{3,5},{4,28},{5,3},{6,30},{7,1},{8,16},{9,15},... | collective-permute-start | bytes 55304 | tf_op jit(solution)/shard_map/ppermute | solution.py:601
  39.2 4.4 %collective-permute-start.8 = (f32[48,96]{1,0:T(8,128)S(1)}, f32[48,96]{1,0:T(8,128)S(1)}, u32[]{:S(2)}, u32[]{:S(2)}) collective-permute-start(f32[48,96]{1,0:T(8,128)S(1)} %add.21), channel_id=1, source_target_pairs={{0,8},{1,5},{2,10},{3,7},{4,12},{5,1},{6,14},{7,3},{8,0},{9,13},{1... | collective-permute-start | bytes 55304 | tf_op jit(solution)/shard_map/ppermute | solution.py:601
  43.7 4.4 %collective-permute-start.12 = (f32[48,96]{1,0:T(8,128)S(1)}, f32[48,96]{1,0:T(8,128)S(1)}, u32[]{:S(2)}, u32[]{:S(2)}) collective-permute-start(f32[48,96]{1,0:T(8,128)S(1)} %add_add_fusion.1), channel_id=1, source_target_pairs={{0,2},{1,17},{2,0},{3,19},{4,6},{5,21},{6,4},{7,23},{8,10},{9,25},... | collective-permute-start | bytes 55304 | tf_op jit(solution)/shard_map/ppermute | solution.py:601
  46.3 4.7 %collective-permute-start.13 = (f32[48,96]{1,0:T(8,128)S(1)}, f32[48,96]{1,0:T(8,128)S(1)}, u32[]{:S(2)}, u32[]{:S(2)}) collective-permute-start(f32[48,96]{1,0:T(8,128)S(1)} %add_add_fusion.1), channel_id=1, source_target_pairs={{0,6},{1,25},{2,4},{3,27},{4,2},{5,29},{6,0},{7,31},{8,14},{9,17},... | collective-permute-start | bytes 55304 | tf_op jit(solution)/shard_map/ppermute | solution.py:601
  47.3 3.8 %collective-permute-start.11 = (f32[48,96]{1,0:T(8,128)S(1)}, f32[48,96]{1,0:T(8,128)S(1)}, u32[]{:S(2)}, u32[]{:S(2)}) collective-permute-start(f32[48,96]{1,0:T(8,128)S(1)} %add_add_fusion.1), channel_id=1, source_target_pairs={{0,4},{1,9},{2,6},{3,11},{4,0},{5,13},{6,2},{7,15},{8,12},{9,1},{1... | collective-permute-start | bytes 55304 | tf_op jit(solution)/shard_map/ppermute | solution.py:601
  51.1 1.3 %collective-permute-start.14 = (f32[48,96]{1,0:T(8,128)S(1)}, f32[48,96]{1,0:T(8,128)S(1)}, u32[]{:S(2)}, u32[]{:S(2)}) collective-permute-start(f32[48,96]{1,0:T(8,128)S(1)} %add_add_fusion.refs_0_), channel_id=1, source_target_pairs={{0,1},{1,0},{2,3},{3,2},{4,5},{5,4},{6,7},{7,6},{8,9},{9,8},{10,11... | collective-permute-start | bytes 55304 | tf_op jit(solution)/shard_map/ppermute | solution.py:759
